TPU v7x, 256 devices: a whole 4x4x8 slice. The times are simulated.
256 devices in a mesh: mrow: 32 (over x_hi, z, core), mcol: 8 (over y, x_lo).
Axes of the slice: x: 4 (x_hi: 2, x_lo: 2; x = x_hi * 2 + x_lo), y: 4, z: 8, core: 2. Of those that a mesh axis runs over, the one named last changes fastest.
Arguments:
- queries: bfloat16 [4096, 4096], P('mrow', 'mcol'), may hold values from -6 to 6
- grad_out: bfloat16 [4096, 4096], P('mrow', 'mcol'), may hold values from -6 to 6
- attn_out: bfloat16 [4096, 4096], P('mrow', 'mcol'), may hold values from -2 to 2
- log_sum: float32 [4096, 32], P('mrow', 'mcol'), as said below
- memory_keys: bfloat16 [256, 128, 1024], P('mrow', 'mcol'), may hold values from -6 to 6
- memory_values: bfloat16 [256, 128, 1024], P('mrow', 'mcol'), may hold values from -6 to 6
Outputs:
- grad_queries: float32 [4096, 4096], P('mrow', 'mcol')
Inputs may be any that keep to these rules, and one draw needn't show every extreme that they name: `log_sum`: each entry is the natural logarithm of 32768, plus 0 to 1.
All inputs are finite; a program needn't handle non-finite values.
Results may differ from a plain program's by a relative error of at most 0.0023.
Values may be sent and summed in bfloat16 or wider, within the bound.
A program may use at most 64 MiB of HBM per device.

v0:
```python
import jax
import jax.numpy as jnp
from jax import lax
from jax.sharding import PartitionSpec as P

H = 32
KVH = 8
HD = 128


def divisor_at_most(total, limit):
    best = 1
    for size in range(1, total + 1):
        if total % size == 0 and size <= limit:
            best = size
    return best


def head_terms(query_heads, grad_heads, log_heads, dot_heads, mem_keys, mem_values):
    scaling = HD ** (-0.5)
    scores = (
        jnp.einsum("tkgd,ekd->kgte", query_heads, mem_keys, preferred_element_type=jnp.float32)
        * scaling
    )
    weights = jnp.exp(scores - log_heads[..., None])
    grad_probs = jnp.einsum(
        "tkgd,ekd->kgte", grad_heads, mem_values, preferred_element_type=jnp.float32
    )
    grad_scores = (weights * (grad_probs - dot_heads[..., None])).astype(jnp.bfloat16)
    return scaling * jnp.einsum(
        "kgte,ekd->tkgd", grad_scores, mem_keys, preferred_element_type=jnp.float32
    )


def block_terms(stacked, log_rows, dot_rows, mem_keys, mem_values):
    row_count = stacked.shape[0]
    heads_here = log_rows.shape[1]
    per_group = H // KVH
    kv_here = heads_here // per_group
    entries = mem_keys.shape[0]
    step = divisor_at_most(row_count, max(1, 2**21 // (heads_here * entries)))
    count = row_count // step
    query_heads = stacked[:, 0].reshape(count, step, kv_here, per_group, HD)
    grad_heads = stacked[:, 1].reshape(count, step, kv_here, per_group, HD)
    log_heads = log_rows.reshape(count, step, kv_here, per_group).transpose(0, 2, 3, 1)
    dot_heads = dot_rows.reshape(count, step, kv_here, per_group).transpose(0, 2, 3, 1)

    def one_block(inputs):
        query_part, grad_part, log_part, dot_part = inputs
        return head_terms(query_part, grad_part, log_part, dot_part, mem_keys, mem_values)

    terms = lax.map(one_block, (query_heads, grad_heads, log_heads, dot_heads))
    return terms.reshape(row_count, heads_here * HD)


def body(queries, grad_out, attn_out, log_sum, memory_keys, memory_values):
    token_count = queries.shape[0]
    heads_here = log_sum.shape[1]
    kv_here = heads_here // (H // KVH)
    out_dot = jnp.sum(
        (grad_out.astype(jnp.float32) * attn_out.astype(jnp.float32)).reshape(
            token_count, heads_here, HD
        ),
        axis=-1,
    )
    key_tiles = memory_keys.reshape(memory_keys.shape[0], memory_keys.shape[1], KVH, HD)
    value_tiles = memory_values.reshape(memory_values.shape[0], memory_values.shape[1], KVH, HD)
    own_keys, own_values = (
        lax.all_to_all(key_tiles, "mcol", split_axis=2, concat_axis=1, tiled=True),
        lax.all_to_all(value_tiles, "mcol", split_axis=2, concat_axis=1, tiled=True),
    )
    mem_keys = own_keys.reshape(-1, kv_here, HD)
    mem_values = own_values.reshape(-1, kv_here, HD)
    stacked = jnp.stack([queries, grad_out], axis=1)
    gathered_stats = (
        lax.all_gather(log_sum, "mrow", axis=0, tiled=True),
        lax.all_gather(out_dot, "mrow", axis=0, tiled=True),
    )
    log_rows = gathered_stats[0]
    dot_rows = gathered_stats[1]
    partial_grad = block_terms(
        lax.all_gather(stacked, "mrow", axis=0, tiled=True),
        log_rows,
        dot_rows,
        mem_keys,
        mem_values,
    )
    result = lax.psum_scatter(partial_grad, "mrow", scatter_dimension=0, tiled=True)
    return result


def solution(mesh):
    return jax.shard_map(
        body,
        mesh=mesh,
        in_specs=(
            P("mrow", "mcol"),
            P("mrow", "mcol"),
            P("mrow", "mcol"),
            P("mrow", "mcol"),
            P("mrow", "mcol", None),
            P("mrow", "mcol", None),
        ),
        out_specs=P("mrow", "mcol"),
        check_vma=False,
    )
```

profile of v0, /device:TPU:16, one launch (start us, length us, event | category | flops | bytes accessed | tf_op | source)
XLA Modules:
  0.0 411.0 jit_solution(14667618074723072190)
XLA Ops:
  6.5 0.0 copy-start
  6.5 0.0 copy-start.1
  6.5 0.0 all-gather.2.cloned.1.call-start
  6.5 1.7 pad_maximum_fusion
  8.3 0.0 all-gather.2.cloned.1.call-update
  8.3 0.0 copy-done
  8.3 0.8 copy_bitcast_fusion.8
  9.1 5.7 %all-to-all-start = ((bf16[8,16,8,128]{3,1,0,2:T(8,128)(2,1)}), bf16[8,16,8,128]{3,1,0,2:T(8,128)(2,1)S(1)}, u32[]{:S(2)}, u32[]{:S(2)}) async-start(bf16[8,16,8,128]{3,1,0,2:T(8,128)(2,1)} %copy_bitcast_fusion.8), calls=%async_computation | async-start | bytes 524288 | tf_op jit(solution)/shard_map/all_to_all | solution.py:69
  14.8 1.7 copy_bitcast_fusion.7
  16.5 3.2 all-to-all-done
  19.7 5.8 %all-to-all-start.1 = ((bf16[8,16,8,128]{3,1,0,2:T(8,128)(2,1)}), bf16[8,16,8,128]{3,1,0,2:T(8,128)(2,1)S(1)}, u32[]{:S(2)}, u32[]{:S(2)}) async-start(bf16[8,16,8,128]{3,1,0,2:T(8,128)(2,1)} %copy_bitcast_fusion.7), calls=%async_computation.1 | async-start | bytes 524288 | tf_op jit(solution)/shard_map/all_to_all | solution.py:70
  25.4 0.0 reduce-scatter.2.cloned.1.call-start
  25.4 1.0 convert_multiply_fusion
  26.4 0.1 reshape.64
  26.5 0.2 reduce_sum.9
  26.7 52.6 %all_gather.11 = f32[4096,4]{1,0:T(8,128)S(1)} all-gather(f32[128,4]{1,0:T(8,128)S(1)} %reduce_sum.9), channel_id=1, replica_groups=mesh['mrow'=32,'mcol'=8] {'mrow'}, dimensions={0}, use_global_device_ids=true | all-gather | bytes 67584 | tf_op jit(solution)/shard_map/all_gather | solution.py:77
  79.4 0.6 copy.40
  80.0 0.0 copy-done.1
  80.0 37.0 %all_gather.10 = f32[4096,4]{0,1:T(4,128)S(1)} all-gather(f32[128,4]{0,1:T(4,128)S(1)} %copy-done.1), channel_id=1, replica_groups=mesh['mrow'=32,'mcol'=8] {'mrow'}, dimensions={0}, use_global_device_ids=true | all-gather | bytes 67584 | tf_op jit(solution)/shard_map/all_gather | solution.py:76
  117.0 0.0 all-to-all-done.1
  117.1 0.0 all-gather.2.cloned.1.call-done
  117.1 5.7 %fusion.20 = (bf16[4096,1,512]{2,0,1:T(8,128)(2,1)}, bf16[4096,1,512]{2,0,1:T(8,128)(2,1)}) fusion(bf16[4096,2,512]{2,0,1:T(8,128)(2,1)} %all-gather.2.cloned.1.call-done), kind=kLoop, calls=%fused_computation.28 | loop fusion | bytes 16777216 | tf_op jit(solution)/shard_map/slice | solution.py:44
  122.8 6.9 %reshape.69 = bf16[8,512,1,4,128]{4,3,1,0,2:T(4,128)(2,1)} reshape(bf16[4096,1,512]{2,0,1:T(8,128)(2,1)} %get-tuple-element.93) | data formatting | bytes 8388608 | tf_op jit(solution)/shard_map/reshape;squeeze | solution.py:43
  129.8 6.9 %reshape.70 = bf16[8,512,1,4,128]{4,3,1,0,2:T(4,128)(2,1)} reshape(bf16[4096,1,512]{2,0,1:T(8,128)(2,1)} %get-tuple-element.92) | data formatting | bytes 8388608 | tf_op jit(solution)/shard_map/reshape;squeeze | solution.py:44
  136.7 108.8 %while.10 = (s32[]{:T(128)}, f32[8,512,1,4,128]{4,3,1,0,2:T(4,128)}, bf16[8,512,1,4,128]{4,3,1,0,2:T(4,128)(2,1)}, bf16[1024,1,128]{2,0,1:T(8,128)(2,1)S(1)}, f3...) while((s32[]{:T(128)}, ...), condition=%wide.region_2.3_spmd, body=%wide.region_1.2_spmd.sunk | while | flops 1621360640 | bytes 23921256 | solution.py:52
  136.7 1.6 constant_dynamic-slice_fusion.5
  138.3 4.5 %fusion.33 = f32[512,4,1024]{2,0,1:T(8,128)} fusion(bf16[1,512,1,4,128]{4,3,1,0,2:T(4,128)(2,1)S(1)} %get-tuple-element.147, bf16[1024,1,128]{2,0,1:T(8,128)(2,1)S(1)} %get-tuple-element.172), kind=kOutput, calls=%fused_computation.13.clone.1 | convolution fusion | flops 536870912 | bytes 9175040 | tf_op jit(solution)/shard_map/while/body/eval_jaxpr/tkgd,ekd->kgte/dot_general | solution.py:22
  142.7 5.8 %fusion.34 = f32[1,512,1,4,128]{4,1,3,2,0:T(8,128)S(1)} fusion(f32[512,4,1024]{2,0,1:T(8,128)} %fusion.33, f32[4,512]{1,0:T(4,128)S(1)} %get-tuple-element.148, f32[4,512]{1,0:T(4,128)S(1)} %get-tuple-element.149, bf16[1,512,1,4,128]{4,3,1,0,2:T(4,128)(2,1)S(1)} %get-tuple-element.150, bf16[1024,1,128]{2,0,1:T(8,128)(2,1)S(1)} %get-tuple-element.175, ...), kind=kOutput, calls=%fused_computation.9.clone.1 | convolution fusion | flops 1084489728 | bytes 10502144 | tf_op jit(solution)/shard_map/while/body/eval_jaxpr/kgte,ekd->tkgd/dot_general | solution.py:30
  148.6 1.7 copy_dynamic-update-slice_fusion.2
  150.3 1.6 constant_dynamic-slice_fusion.5
  151.8 4.5 %fusion.33 = f32[512,4,1024]{2,0,1:T(8,128)} fusion(bf16[1,512,1,4,128]{4,3,1,0,2:T(4,128)(2,1)S(1)} %get-tuple-element.147, bf16[1024,1,128]{2,0,1:T(8,128)(2,1)S(1)} %get-tuple-element.172), kind=kOutput, calls=%fused_computation.13.clone.1 | convolution fusion | flops 536870912 | bytes 9175040 | tf_op jit(solution)/shard_map/while/body/eval_jaxpr/tkgd,ekd->kgte/dot_general | solution.py:22
  156.3 5.8 %fusion.34 = f32[1,512,1,4,128]{4,1,3,2,0:T(8,128)S(1)} fusion(f32[512,4,1024]{2,0,1:T(8,128)} %fusion.33, f32[4,512]{1,0:T(4,128)S(1)} %get-tuple-element.148, f32[4,512]{1,0:T(4,128)S(1)} %get-tuple-element.149, bf16[1,512,1,4,128]{4,3,1,0,2:T(4,128)(2,1)S(1)} %get-tuple-element.150, bf16[1024,1,128]{2,0,1:T(8,128)(2,1)S(1)} %get-tuple-element.175, ...), kind=kOutput, calls=%fused_computation.9.clone.1 | convolution fusion | flops 1084489728 | bytes 10502144 | tf_op jit(solution)/shard_map/while/body/eval_jaxpr/kgte,ekd->tkgd/dot_general | solution.py:30
  162.2 1.7 copy_dynamic-update-slice_fusion.2
  163.9 1.6 constant_dynamic-slice_fusion.5
  165.5 4.5 %fusion.33 = f32[512,4,1024]{2,0,1:T(8,128)} fusion(bf16[1,512,1,4,128]{4,3,1,0,2:T(4,128)(2,1)S(1)} %get-tuple-element.147, bf16[1024,1,128]{2,0,1:T(8,128)(2,1)S(1)} %get-tuple-element.172), kind=kOutput, calls=%fused_computation.13.clone.1 | convolution fusion | flops 536870912 | bytes 9175040 | tf_op jit(solution)/shard_map/while/body/eval_jaxpr/tkgd,ekd->kgte/dot_general | solution.py:22
  169.9 5.8 %fusion.34 = f32[1,512,1,4,128]{4,1,3,2,0:T(8,128)S(1)} fusion(f32[512,4,1024]{2,0,1:T(8,128)} %fusion.33, f32[4,512]{1,0:T(4,128)S(1)} %get-tuple-element.148, f32[4,512]{1,0:T(4,128)S(1)} %get-tuple-element.149, bf16[1,512,1,4,128]{4,3,1,0,2:T(4,128)(2,1)S(1)} %get-tuple-element.150, bf16[1024,1,128]{2,0,1:T(8,128)(2,1)S(1)} %get-tuple-element.175, ...), kind=kOutput, calls=%fused_computation.9.clone.1 | convolution fusion | flops 1084489728 | bytes 10502144 | tf_op jit(solution)/shard_map/while/body/eval_jaxpr/kgte,ekd->tkgd/dot_general | solution.py:30
  175.8 1.7 copy_dynamic-update-slice_fusion.2
  177.5 1.6 constant_dynamic-slice_fusion.5
  179.1 4.5 %fusion.33 = f32[512,4,1024]{2,0,1:T(8,128)} fusion(bf16[1,512,1,4,128]{4,3,1,0,2:T(4,128)(2,1)S(1)} %get-tuple-element.147, bf16[1024,1,128]{2,0,1:T(8,128)(2,1)S(1)} %get-tuple-element.172), kind=kOutput, calls=%fused_computation.13.clone.1 | convolution fusion | flops 536870912 | bytes 9175040 | tf_op jit(solution)/shard_map/while/body/eval_jaxpr/tkgd,ekd->kgte/dot_general | solution.py:22
  183.5 5.8 %fusion.34 = f32[1,512,1,4,128]{4,1,3,2,0:T(8,128)S(1)} fusion(f32[512,4,1024]{2,0,1:T(8,128)} %fusion.33, f32[4,512]{1,0:T(4,128)S(1)} %get-tuple-element.148, f32[4,512]{1,0:T(4,128)S(1)} %get-tuple-element.149, bf16[1,512,1,4,128]{4,3,1,0,2:T(4,128)(2,1)S(1)} %get-tuple-element.150, bf16[1024,1,128]{2,0,1:T(8,128)(2,1)S(1)} %get-tuple-element.175, ...), kind=kOutput, calls=%fused_computation.9.clone.1 | convolution fusion | flops 1084489728 | bytes 10502144 | tf_op jit(solution)/shard_map/while/body/eval_jaxpr/kgte,ekd->tkgd/dot_general | solution.py:30
  189.4 1.7 copy_dynamic-update-slice_fusion.2
  191.1 1.6 constant_dynamic-slice_fusion.5
  192.7 4.5 %fusion.33 = f32[512,4,1024]{2,0,1:T(8,128)} fusion(bf16[1,512,1,4,128]{4,3,1,0,2:T(4,128)(2,1)S(1)} %get-tuple-element.147, bf16[1024,1,128]{2,0,1:T(8,128)(2,1)S(1)} %get-tuple-element.172), kind=kOutput, calls=%fused_computation.13.clone.1 | convolution fusion | flops 536870912 | bytes 9175040 | tf_op jit(solution)/shard_map/while/body/eval_jaxpr/tkgd,ekd->kgte/dot_general | solution.py:22
  197.1 5.8 %fusion.34 = f32[1,512,1,4,128]{4,1,3,2,0:T(8,128)S(1)} fusion(f32[512,4,1024]{2,0,1:T(8,128)} %fusion.33, f32[4,512]{1,0:T(4,128)S(1)} %get-tuple-element.148, f32[4,512]{1,0:T(4,128)S(1)} %get-tuple-element.149, bf16[1,512,1,4,128]{4,3,1,0,2:T(4,128)(2,1)S(1)} %get-tuple-element.150, bf16[1024,1,128]{2,0,1:T(8,128)(2,1)S(1)} %get-tuple-element.175, ...), kind=kOutput, calls=%fused_computation.9.clone.1 | convolution fusion | flops 1084489728 | bytes 10502144 | tf_op jit(solution)/shard_map/while/body/eval_jaxpr/kgte,ekd->tkgd/dot_general | solution.py:30
  203.0 1.6 copy_dynamic-update-slice_fusion.2
  204.7 1.6 constant_dynamic-slice_fusion.5
  206.2 4.5 %fusion.33 = f32[512,4,1024]{2,0,1:T(8,128)} fusion(bf16[1,512,1,4,128]{4,3,1,0,2:T(4,128)(2,1)S(1)} %get-tuple-element.147, bf16[1024,1,128]{2,0,1:T(8,128)(2,1)S(1)} %get-tuple-element.172), kind=kOutput, calls=%fused_computation.13.clone.1 | convolution fusion | flops 536870912 | bytes 9175040 | tf_op jit(solution)/shard_map/while/body/eval_jaxpr/tkgd,ekd->kgte/dot_general | solution.py:22
  210.7 5.8 %fusion.34 = f32[1,512,1,4,128]{4,1,3,2,0:T(8,128)S(1)} fusion(f32[512,4,1024]{2,0,1:T(8,128)} %fusion.33, f32[4,512]{1,0:T(4,128)S(1)} %get-tuple-element.148, f32[4,512]{1,0:T(4,128)S(1)} %get-tuple-element.149, bf16[1,512,1,4,128]{4,3,1,0,2:T(4,128)(2,1)S(1)} %get-tuple-element.150, bf16[1024,1,128]{2,0,1:T(8,128)(2,1)S(1)} %get-tuple-element.175, ...), kind=kOutput, calls=%fused_computation.9.clone.1 | convolution fusion | flops 1084489728 | bytes 10502144 | tf_op jit(solution)/shard_map/while/body/eval_jaxpr/kgte,ekd->tkgd/dot_general | solution.py:30
  216.5 1.7 copy_dynamic-update-slice_fusion.2
  218.3 1.6 constant_dynamic-slice_fusion.5
  219.8 4.5 %fusion.33 = f32[512,4,1024]{2,0,1:T(8,128)} fusion(bf16[1,512,1,4,128]{4,3,1,0,2:T(4,128)(2,1)S(1)} %get-tuple-element.147, bf16[1024,1,128]{2,0,1:T(8,128)(2,1)S(1)} %get-tuple-element.172), kind=kOutput, calls=%fused_computation.13.clone.1 | convolution fusion | flops 536870912 | bytes 9175040 | tf_op jit(solution)/shard_map/while/body/eval_jaxpr/tkgd,ekd->kgte/dot_general | solution.py:22
  224.3 5.8 %fusion.34 = f32[1,512,1,4,128]{4,1,3,2,0:T(8,128)S(1)} fusion(f32[512,4,1024]{2,0,1:T(8,128)} %fusion.33, f32[4,512]{1,0:T(4,128)S(1)} %get-tuple-element.148, f32[4,512]{1,0:T(4,128)S(1)} %get-tuple-element.149, bf16[1,512,1,4,128]{4,3,1,0,2:T(4,128)(2,1)S(1)} %get-tuple-element.150, bf16[1024,1,128]{2,0,1:T(8,128)(2,1)S(1)} %get-tuple-element.175, ...), kind=kOutput, calls=%fused_computation.9.clone.1 | convolution fusion | flops 1084489728 | bytes 10502144 | tf_op jit(solution)/shard_map/while/body/eval_jaxpr/kgte,ekd->tkgd/dot_general | solution.py:30
  230.1 1.7 copy_dynamic-update-slice_fusion.2
  231.9 1.6 constant_dynamic-slice_fusion.5
  233.4 4.5 %fusion.33 = f32[512,4,1024]{2,0,1:T(8,128)} fusion(bf16[1,512,1,4,128]{4,3,1,0,2:T(4,128)(2,1)S(1)} %get-tuple-element.147, bf16[1024,1,128]{2,0,1:T(8,128)(2,1)S(1)} %get-tuple-element.172), kind=kOutput, calls=%fused_computation.13.clone.1 | convolution fusion | flops 536870912 | bytes 9175040 | tf_op jit(solution)/shard_map/while/body/eval_jaxpr/tkgd,ekd->kgte/dot_general | solution.py:22
  237.9 5.8 %fusion.34 = f32[1,512,1,4,128]{4,1,3,2,0:T(8,128)S(1)} fusion(f32[512,4,1024]{2,0,1:T(8,128)} %fusion.33, f32[4,512]{1,0:T(4,128)S(1)} %get-tuple-element.148, f32[4,512]{1,0:T(4,128)S(1)} %get-tuple-element.149, bf16[1,512,1,4,128]{4,3,1,0,2:T(4,128)(2,1)S(1)} %get-tuple-element.150, bf16[1024,1,128]{2,0,1:T(8,128)(2,1)S(1)} %get-tuple-element.175, ...), kind=kOutput, calls=%fused_computation.9.clone.1 | convolution fusion | flops 1084489728 | bytes 10502144 | tf_op jit(solution)/shard_map/while/body/eval_jaxpr/kgte,ekd->tkgd/dot_general | solution.py:30
  243.8 1.7 copy_dynamic-update-slice_fusion.2
  245.5 7.6 %copy.60 = f32[512,8,4,128]{3,1,2,0:T(8,128)} copy(f32[512,8,4,128]{3,2,1,0:T(4,128)} %bitcast.130) | data formatting | bytes 16777216
  253.1 0.0 reduce-scatter.2.cloned.1.call-update
  253.1 151.1 %reduce-scatter.2.cloned.1.call-done = f32[128,512]{1,0:T(8,128)} async-done(((f32[4096,512]{1,0:T(8,128)}), f32[128,512]{1,0:T(8,128)}) %reduce-scatter.2.cloned.1.call-update) | async-done | bytes 262160 | tf_op jit(solution)/shard_map/reduce_scatter | solution.py:88
  (19 shorter events, 0.2 us)
Async XLA Ops:
  6.5 1.8 copy-start
  6.5 73.5 %copy-start.1 = (f32[128,4]{0,1:T(4,128)S(1)}, f32[128,4]{0,1:T(4,128)}, u32[]{:S(2)}) copy-start(f32[128,4]{0,1:T(4,128)} %param.11) | copy-start | bytes 6148
  6.5 110.6 %all-gather.2.cloned.1.call-start = ((), (), s32[]{:S(2)}) async-start(), calls=%async_computation.3 | async-start | bytes 8650752 | tf_op jit(solution)/shard_map/all_gather | solution.py:82
  9.1 10.6 %all-to-all-start = ((bf16[8,16,8,128]{3,1,0,2:T(8,128)(2,1)}), bf16[8,16,8,128]{3,1,0,2:T(8,128)(2,1)S(1)}, u32[]{:S(2)}, u32[]{:S(2)}) async-start(bf16[8,16,8,128]{3,1,0,2:T(8,128)(2,1)} %copy_bitcast_fusion.8), calls=%async_computation | async-start | bytes 524288 | tf_op jit(solution)/shard_map/all_to_all | solution.py:69
  19.7 97.4 %all-to-all-start.1 = ((bf16[8,16,8,128]{3,1,0,2:T(8,128)(2,1)}), bf16[8,16,8,128]{3,1,0,2:T(8,128)(2,1)S(1)}, u32[]{:S(2)}, u32[]{:S(2)}) async-start(bf16[8,16,8,128]{3,1,0,2:T(8,128)(2,1)} %copy_bitcast_fusion.7), calls=%async_computation.1 | async-start | bytes 524288 | tf_op jit(solution)/shard_map/all_to_all | solution.py:70
  25.4 378.7 %reduce-scatter.2.cloned.1.call-start = ((), (), s32[]{:S(2)}) async-start(), calls=%async_computation.4 | async-start | bytes 8650752 | tf_op jit(solution)/shard_map/reduce_scatter | solution.py:88
Sparse Core Ops, SparseCore 0:
  10.2 106.6 all-gather.1
  253.2 150.9 reduce-scatter.1
where the time goes:
time: 412 us; the launch traced here: 411 us
  waiting for transfers between devices  154 us (37%)
  blocking collectives  89.6 us (22%)
  matrix products  82.5 us (20%)
  local copies, waits for them, and re-layouts  56.5 us (14%)
  between operations  13.5 us (3%)
  starting transfers between devices  11.5 us (3%)
    reduce_scatter x1, waiting for transfers between devices, body(): lax.psum_scatter(partial_grad, 'mrow', scatter_dimension=0, tiled=True)  151 us
    all_gather x1, blocking collectives, body(): lax.all_gather(out_dot, 'mrow', axis=0, tiled=True)  52.6 us
    dot_general x8, matrix products, head_terms(): jnp.einsum('kgte,ekd->tkgd', grad_scores, mem_keys, preferred_element_typ...  46.7 us
    all_gather x1, blocking collectives, body(): lax.all_gather(log_sum, 'mrow', axis=0, tiled=True)  37 us
    dot_general x8, matrix products, head_terms(): jnp.einsum('tkgd,ekd->kgte', query_heads, mem_keys, preferred_element_typ...  35.8 us
    dynamic_update_slice x8, local copies, waits for them, and re-layouts, block_terms(): terms = lax.map(one_block, (query_heads, grad_heads, log_heads, dot_heads))  13.4 us
    dynamic_slice x16, local copies, waits for them, and re-layouts, block_terms(): terms = lax.map(one_block, (query_heads, grad_heads, log_heads, dot_heads))  12.6 us
  transfers between devices with their start and end apart: 4, of which 2 were waited for; matrix products, arithmetic and copies ran while one was open for 1% of the time, Pallas kernels for 0%

commit v1 on v0

v1 whole, which is shorter than its diff:
```python
import jax
import jax.numpy as jnp
from jax import lax
from jax.experimental import pallas as pl
from jax.experimental.pallas import tpu as pltpu
from jax.sharding import PartitionSpec as P

H = 32
KVH = 8
HD = 128
SCALE = HD ** -0.5
LOG2E = 1.4426950408889634
ZN = 8
F32 = jnp.float32
BF16 = jnp.bfloat16
MESH = pl.DeviceIdType.MESH
NT = (((1,), (1,)), ((), ()))
NN = (((1,), (0,)), ((), ()))

UNITS = (
    ((0, 0), (1, 0)),
    ((0, 1), (0, 7)),
    ((0, 2), (0, 6)),
    ((0, 3), (0, 5)),
    ((0, 4), (1, 4)),
    ((1, 3), (1, 5)),
    ((1, 2), (1, 6)),
    ((1, 1), (1, 7)),
)
POS = {block: 2 * u + i for u, unit in enumerate(UNITS) for i, block in enumerate(unit)}
UP, DOWN = 0, 1
GATHER = {(UP, 0): (0, 1, 2, 3), (UP, 1): (0, 1, 2), (DOWN, 0): (0, 7, 6), (DOWN, 1): (0, 7, 6, 5)}
REDUCE = {(DOWN, 0): (4, 3, 2, 1), (DOWN, 1): (3, 2, 1), (UP, 0): (5, 6, 7), (UP, 1): (4, 5, 6, 7)}
MESSAGES = [(d, hp, slot) for (d, hp), slots in REDUCE.items() for slot in slots]
MSG = {message: i for i, message in enumerate(MESSAGES)}
ROWS = 272
STEPS = 16


def kernel(
    l_ref, q_hbm, g_hbm, a_hbm, k_hbm, v_hbm, out_ref,
    qg, kv, kt, acc, abuf, sbuf, rbuf,
    local_sem, a2a_send, a2a_recv, fwd_send, fwd_recv, ring_send, ring_recv, red_send, red_recv,
):
    r, m = lax.axis_index("mrow"), lax.axis_index("mcol")
    xh, z, c = lax.div(r, 2 * ZN), lax.rem(lax.div(r, 2), ZN), lax.rem(r, 2)
    other = (1 - xh) * (2 * ZN) + z * 2 + c
    sibling = xh * (2 * ZN) + z * 2 + 1 - c
    above = xh * (2 * ZN) + lax.rem(z + 1, ZN) * 2 + c
    below = xh * (2 * ZN) + lax.rem(z + ZN - 1, ZN) * 2 + c
    toward = {UP: above, DOWN: below}

    def col(mr):
        return lax.rem(m + mr, KVH)

    def head_lanes(j):
        return pl.ds(pl.multiple_of(j * HD, HD), HD)

    local = []
    for hp in range(2):
        lanes = pl.ds(hp * 256, 256)
        local.append((q_hbm.at[:, lanes], qg.at[POS[hp, 0], pl.ds(0, 128)]))
        local.append((g_hbm.at[:, lanes], qg.at[POS[hp, 0], pl.ds(128, 128)]))
    local.append((a_hbm, abuf))
    local.append((k_hbm.at[:, head_lanes(m)], kv.at[0, 0]))
    local.append((v_hbm.at[:, head_lanes(m)], kv.at[1, 0]))
    local = [pltpu.make_async_copy(s, d, local_sem.at[i]) for i, (s, d) in enumerate(local)]
    for copy in local:
        copy.start()

    barrier = pltpu.get_barrier_semaphore()
    peers = [(r, col(mr)) for mr in range(1, KVH)] + [(other, col(mr)) for mr in range(KVH)]
    peers += [(sibling, m), (above, m), (below, m)]
    for peer in peers:
        pl.semaphore_signal(barrier, inc=1, device_id=peer, device_id_type=MESH)
    pl.semaphore_wait(barrier, len(peers))

    a2a = []
    for xr in range(2):
        for mr in range(1 - xr, KVH):
            for i, hbm in enumerate((k_hbm, v_hbm)):
                copy = pltpu.make_async_remote_copy(
                    src_ref=hbm.at[:, head_lanes(col(mr))],
                    dst_ref=kv.at[i, xr * 16 + (KVH - mr) % KVH],
                    send_sem=a2a_send.at[xr, i, mr],
                    recv_sem=a2a_recv.at[xr, i],
                    device_id=(other if xr else r, col(mr)),
                    device_id_type=MESH,
                )
                copy.start()
                a2a.append(copy)

    for copy in local[:5]:
        copy.wait()
    lane = lax.broadcasted_iota(jnp.int32, (128, 128), 1)
    stats = jnp.zeros((128, 128), F32)
    for h in range(4):
        hp, hl = h // 2, h % 2
        grad = qg[POS[hp, 0], 128:256, hl * 128 : hl * 128 + 128].astype(F32)
        attn = abuf[:, h * 128 : h * 128 + 128].astype(F32)
        stats = jnp.where(lane == h, l_ref[:, h : h + 1] * LOG2E, stats)
        stats = jnp.where(lane == 4 + h, jnp.sum(grad * attn, axis=1, keepdims=True), stats)
    stats = stats.T
    row = lax.broadcasted_iota(jnp.int32, (16, 256), 0)
    for hp in range(2):
        packed = jnp.zeros((16, 256), F32)
        for i in range(2):
            rest = jnp.concatenate([stats[4 * i + 2 * hp + hl : 4 * i + 2 * hp + hl + 1] for hl in range(2)], axis=1)
            for piece in range(3):
                part = rest.astype(BF16).astype(F32)
                packed = jnp.where(row == 3 * i + piece, part, packed)
                rest = rest - part
        qg[POS[hp, 0], 256:272, :] = packed.astype(BF16)

    def ring(d, hp, hop):
        slot = GATHER[d, hp][hop]
        landing = (slot + 1) % ZN if d == UP else (slot + ZN - 1) % ZN
        return pltpu.make_async_remote_copy(
            src_ref=qg.at[POS[hp, slot]],
            dst_ref=qg.at[POS[hp, landing]],
            send_sem=ring_send.at[d, hp, hop],
            recv_sem=ring_recv.at[d, hp, hop],
            device_id=(toward[d], m),
            device_id_type=MESH,
        )

    def pass_on(hp, hop):
        for d in (UP, DOWN):
            hops = len(GATHER[d, hp])
            if hop > 0 and hop <= hops:
                ring(d, hp, hop - 1).wait_recv()
            if hop < hops:
                ring(d, hp, hop).start()

    pass_on(0, 0)
    pass_on(1, 0)

    def forward(xr):
        return pltpu.make_async_remote_copy(
            src_ref=kv.at[:, pl.ds(xr * 16, 8)],
            dst_ref=kv.at[:, pl.ds(xr * 16 + 8, 8)],
            send_sem=fwd_send.at[xr],
            recv_sem=fwd_recv.at[xr],
            device_id=(sibling, m),
            device_id_type=MESH,
        )

    def send_forward(xr):
        for i in range(2):
            got = kv.at[i, pl.ds(xr * 16 + 1 - xr, 7 + xr)]
            pltpu.make_async_copy(got, got, a2a_recv.at[xr, i]).wait()
        forward(xr).start()

    def turn(first):
        def one(s, _):
            kt[first + s] = kv[0, first + s].T
            return 0

        lax.fori_loop(0, 8, one, 0)

    def take_forward(xr):
        turn(xr * 16)
        forward(xr).wait_recv()
        turn(xr * 16 + 8)

    def zero(i, _):
        acc[i] = jnp.zeros((128, 256), F32)
        return 0

    lax.fori_loop(0, 16, zero, 0)
    for copy in local[5:]:
        copy.wait()
    send_forward(0)
    pass_on(0, 1)
    take_forward(0)

    def reduce_copy(d, hp, slot):
        i = MSG[d, hp, slot]
        return pltpu.make_async_remote_copy(
            src_ref=sbuf.at[i],
            dst_ref=rbuf.at[i],
            send_sem=red_send.at[i],
            recv_sem=red_recv.at[i],
            device_id=(toward[d], m),
            device_id_type=MESH,
        )

    def send_sum(d, hp, slot):
        total = acc[POS[hp, slot]]
        before = (d, hp, slot + 1 if d == DOWN else slot - 1)
        if before in MSG:
            reduce_copy(*before).wait_recv()
            total = total + rbuf[MSG[before]].astype(F32)
        sbuf[MSG[d, hp, slot]] = total.astype(BF16)
        reduce_copy(d, hp, slot).start()

    def finish(hp):
        total = acc[POS[hp, 0]]
        for last in ((DOWN, hp, 1), (UP, hp, 7)):
            reduce_copy(*last).wait_recv()
            total = total + rbuf[MSG[last]].astype(F32)
        total = total * SCALE
        for hl in range(2):
            h = 2 * hp + hl
            out_ref[:, h * 128 : h * 128 + 128] = total[:, hl * 128 : hl * 128 + 128].T

    def work(u, half):
        first = half * 16
        ks = kv[0, pl.ds(first, 16)].reshape(16 * 128, HD)
        vs = kv[1, pl.ds(first, 16)].reshape(16 * 128, HD)
        blocks = [qg[2 * u], qg[2 * u + 1]]
        qs = jnp.concatenate([b[0:128, i : i + 128] for b in blocks for i in (0, 128)], axis=0)
        gs = jnp.concatenate([b[128:256, i : i + 128] for b in blocks for i in (0, 128)], axis=0)
        st = jnp.concatenate([b[256:272] for b in blocks], axis=1).astype(F32)
        logs = st[0:1] + st[1:2] + st[2:3]
        dots = st[3:4] + st[4:5] + st[5:6]
        scores = lax.dot_general(ks, qs, NT, preferred_element_type=F32)
        probs = lax.dot_general(vs, gs, NT, preferred_element_type=F32)
        ds = (jnp.exp2(scores * (SCALE * LOG2E) - logs) * (probs - dots)).astype(BF16)
        keys = jnp.concatenate([kt[first + i] for i in range(16)], axis=1)
        part = lax.dot_general(keys, ds, NN, preferred_element_type=F32)
        acc[2 * u] += part[:, :256]
        acc[2 * u + 1] += part[:, 256:]

    events = {
        0: [(pass_on, 1, 1)],
        1: [(pass_on, 0, 2), (send_forward, 1)],
        2: [(take_forward, 1), (pass_on, 1, 2)],
        4: [(pass_on, 0, 3)],
        5: [(pass_on, 1, 3)],
        7: [(pass_on, 0, 4), (pass_on, 1, 4), (send_sum, UP, 0, 5)],
        9: [(send_sum, DOWN, 0, 4), (send_sum, UP, 1, 4), (send_sum, UP, 0, 6)],
        11: [
            (send_sum, UP, 1, 5), (send_sum, DOWN, 0, 3), (send_sum, DOWN, 1, 3), (send_sum, UP, 0, 7),
        ],
        13: [(send_sum, UP, 1, 6), (send_sum, DOWN, 1, 2), (send_sum, DOWN, 0, 2)],
        14: [(send_sum, DOWN, 0, 1)],
        15: [(send_sum, UP, 1, 7), (send_sum, DOWN, 1, 1)],
    }

    def one_step(i, _):
        u = jnp.where(i < 3, i, jnp.where(i < 6, i - 3, lax.div(i, 2)))
        half = jnp.where(i < 3, 0, jnp.where(i < 6, 1, lax.rem(i, 2)))
        work(u, half)
        for when, calls in events.items():
            @pl.when(i == when)
            def _(calls=calls):
                for call in calls:
                    call[0](*call[1:])
        return 0

    lax.fori_loop(0, STEPS, one_step, 0)
    finish(0)
    finish(1)

    for copy in a2a:
        copy.wait_send()
    for xr in range(2):
        forward(xr).wait_send()
    for (d, hp), hops in GATHER.items():
        for hop in range(len(hops)):
            ring(d, hp, hop).wait_send()
    for message in MESSAGES:
        reduce_copy(*message).wait_send()


def body(queries, grad_out, attn_out, log_sum, memory_keys, memory_values):
    entries = memory_keys.shape[0] * memory_keys.shape[1]
    any_space = pl.BlockSpec(memory_space=pl.ANY)
    in_vmem = pl.BlockSpec(memory_space=pltpu.VMEM)
    return pl.pallas_call(
        kernel,
        out_shape=jax.ShapeDtypeStruct(queries.shape, F32),
        in_specs=[in_vmem] + [any_space] * 5,
        out_specs=in_vmem,
        scratch_shapes=[
            pltpu.VMEM((16, ROWS, 256), BF16),
            pltpu.VMEM((2, 32, 128, HD), BF16),
            pltpu.VMEM((32, HD, 128), BF16),
            pltpu.VMEM((16, HD, 256), F32),
            pltpu.VMEM((128, 512), BF16),
            pltpu.VMEM((len(MESSAGES), HD, 256), BF16),
            pltpu.VMEM((len(MESSAGES), HD, 256), BF16),
            pltpu.SemaphoreType.DMA((7,)),
            pltpu.SemaphoreType.DMA((2, 2, KVH)),
            pltpu.SemaphoreType.DMA((2, 2)),
            pltpu.SemaphoreType.DMA((2,)),
            pltpu.SemaphoreType.DMA((2,)),
            pltpu.SemaphoreType.DMA((2, 2, 4)),
            pltpu.SemaphoreType.DMA((2, 2, 4)),
            pltpu.SemaphoreType.DMA((len(MESSAGES),)),
            pltpu.SemaphoreType.DMA((len(MESSAGES),)),
        ],
        compiler_params=pltpu.CompilerParams(
            collective_id=0, has_side_effects=True, vmem_limit_bytes=60 << 20
        ),
        cost_estimate=pl.CostEstimate(flops=12884901888, bytes_accessed=2 << 20, transcendentals=16777216),
    )(
        log_sum,
        queries,
        grad_out,
        attn_out,
        memory_keys.reshape(entries, KVH * HD),
        memory_values.reshape(entries, KVH * HD),
    )


def solution(mesh):
    return jax.shard_map(
        body,
        mesh=mesh,
        in_specs=(
            P("mrow", "mcol"),
            P("mrow", "mcol"),
            P("mrow", "mcol"),
            P("mrow", "mcol"),
            P("mrow", "mcol", None),
            P("mrow", "mcol", None),
        ),
        out_specs=P("mrow", "mcol"),
        check_vma=False,
    )
```

time: 412 us -> 72.3 us (0.18)
  waiting for transfers between devices: 154 us -> 0 us
  blocking collectives: 89.6 us -> 0 us
  matrix products: 82.5 us -> 0 us
  Pallas kernels: 0 us -> 69 us
  local copies, waits for them, and re-layouts: 56.5 us -> 3.09 us
  between operations: 13.5 us -> 0.01 us
  starting transfers between devices: 11.5 us -> 0 us
    reduce_scatter x1 -> x0, waiting for transfers between devices: 151 us -> none  [body(): lax.psum_scatter(partial_grad, 'mrow', scatter_dimension=0, tiled=True)]
    all_gather x2 -> x0, blocking collectives: 89.6 us -> none  [the longest x1 52.6 us: body(): lax.all_gather(out_dot, 'mrow', axis=0, tiled=True)]
    dot_general x16 -> x0, matrix products: 82.5 us -> none  [the longest x8 46.7 us: head_terms(): jnp.einsum('kgte,ekd->tkgd', grad_scores, mem_keys, preferred_element_typ...]
    pallas_call x0 -> x1, Pallas kernels: none -> 69 us  [body(): pl.pallas_call(kernel, out_shape=jax.ShapeDtypeStruct(queries.shape, F32)...]
    another operation x2 -> x0, local copies, waits for them, and re-layouts: 13.8 us -> none  [the longest x1 6.91 us: block_terms(): query_heads = stacked[:, 0].reshape(count, step, kv_here, per_group, HD)]
    dynamic_update_slice x8 -> x0, local copies, waits for them, and re-layouts: 13.4 us -> none  [block_terms(): terms = lax.map(one_block, (query_heads, grad_heads, log_heads, dot_heads))]
    dynamic_slice x16 -> x0, local copies, waits for them, and re-layouts: 12.6 us -> none  [block_terms(): terms = lax.map(one_block, (query_heads, grad_heads, log_heads, dot_heads))]
    all_to_all x2 -> x0, starting transfers between devices: 11.5 us -> none  [the longest x1 5.75 us: body(): lax.all_to_all(value_tiles, 'mcol', split_axis=2, concat_axis=1, tiled=True)]
  transfers between devices with their start and end apart: 4 -> 0, of which waited for: 2 -> 0; matrix products, arithmetic and copies ran while one was open for 1% -> 0% of each run, Pallas kernels for 0% -> 0%
where the time goes in v1:
time: 72.3 us; the launch traced here: 72.2 us
  Pallas kernels  69 us (95%)
  local copies, waits for them, and re-layouts  3.09 us (4%)
    pallas_call x1, Pallas kernels, body(): pl.pallas_call(kernel, out_shape=jax.ShapeDtypeStruct(queries.shape, F32)...  69 us
    unnamed x4, local copies, waits for them, and re-layouts  3.09 us

profile of v1, /device:TPU:16, one launch (start us, length us, event | category | flops | bytes accessed | tf_op | source)
XLA Modules:
  0.0 72.2 jit_solution(9068913871602687246)
XLA Ops:
  0.0 0.0 copy-start
  0.0 0.7 copy-done
  0.7 0.7 %copy.7.l_ref = f32[128,4]{1,0:T(8,128)} copy(f32[128,4]{0,1:T(4,128)S(1)} %copy-done) | data formatting | bytes 4096 | tf_op args[3]
  1.4 69.0 %shard_map.64 = f32[128,512]{1,0:T(8,128)} custom-call(f32[128,4]{1,0:T(8,128)} %copy.7.l_ref, bf16[128,512]{1,0:T(8,128)(2,1)} %q_hbm.1, bf16[128,512]{1,0:T(8,128)(2,1)} %g_hbm.1, bf16[128,512]{1,0:T(8,128)(2,1)} %a_hbm.1, bf16[128,1024]{1,0:T(8,128)(2,1)} %bitcast.2, bf16[128,1024]{1,0:T(8,128)(2,1)} %bitcast.3), custom_call_target="tpu_custom_call" | custom-call | flops 12884901888 | bytes 2097152 | tf_op jit(solution)/shard_map/pallas_call | solution.py:271
  70.5 1.7 %copy.9 = f32[128,512]{1,0:T(8,128)} copy(f32[128,512]{1,0:T(8,128)} %shard_map.64) | data formatting | bytes 524288
Async XLA Ops:
  0.0 0.7 copy-start

commit v2 on v1

v2 whole, which is shorter than its diff:
```python
import jax
import jax.numpy as jnp
from jax import lax
from jax.experimental import pallas as pl
from jax.experimental.pallas import tpu as pltpu
from jax.sharding import PartitionSpec as P

H = 32
KVH = 8
HD = 128
SCALE = HD ** -0.5
LOG2E = 1.4426950408889634
ZN = 8
F32 = jnp.float32
BF16 = jnp.bfloat16
MESH = pl.DeviceIdType.MESH
NT = (((1,), (1,)), ((), ()))
NN = (((1,), (0,)), ((), ()))

UNITS = (
    ((0, 0), (1, 0)),
    ((0, 1), (0, 7)),
    ((1, 1), (1, 7)),
    ((0, 2), (0, 6)),
    ((1, 2), (1, 6)),
    ((0, 3), (0, 5)),
    ((1, 3), (1, 5)),
    ((0, 4), (1, 4)),
)
POS = {block: 2 * u + i for u, unit in enumerate(UNITS) for i, block in enumerate(unit)}
UP, DOWN, FAR = 0, 1, 2
GATHER = {(UP, 0): (0, 1, 2, 3), (UP, 1): (0, 1, 2), (DOWN, 0): (0, 7, 6), (DOWN, 1): (0, 7, 6, 5)}
REDUCE = {(DOWN, 0): (3, 2, 1), (DOWN, 1): (3, 2, 1), (UP, 0): (5, 6, 7), (UP, 1): (5, 6, 7), (FAR, 0): (4,), (FAR, 1): (4,)}
MESSAGES = [(d, hp, slot) for (d, hp), slots in REDUCE.items() for slot in slots]
MSG = {message: i for i, message in enumerate(MESSAGES)}
ROWS = 272
STEP_UNIT = (0, 1, 2, 3, 4, 5, 6, 5, 6, 3, 4, 7, 7, 1, 2, 0)
STEP_HALF = (0, 0, 0, 0, 0, 0, 0, 1, 1, 1, 1, 0, 1, 1, 1, 1)


def pick(i, table):
    value = table[-1]
    for k in reversed(range(len(table) - 1)):
        value = jnp.where(i <= k, table[k], value)
    return value


def kernel(
    q_hbm, g_hbm, a_hbm, l_hbm, k_hbm, v_hbm, out_ref,
    qg, kv, kt, acc, abuf, lbuf, sbuf, rbuf,
    local_sem, a2a_send, a2a_recv, relay_send, relay_recv, fwd_send, fwd_recv, ring_send, ring_recv, red_send, red_recv,
):
    r, m = lax.axis_index("mrow"), lax.axis_index("mcol")
    xh, z, c = lax.div(r, 2 * ZN), lax.rem(lax.div(r, 2), ZN), lax.rem(r, 2)
    other = (1 - xh) * (2 * ZN) + z * 2 + c
    sibling = xh * (2 * ZN) + z * 2 + 1 - c
    above = xh * (2 * ZN) + lax.rem(z + 1, ZN) * 2 + c
    below = xh * (2 * ZN) + lax.rem(z + ZN - 1, ZN) * 2 + c
    far = xh * (2 * ZN) + lax.rem(z + ZN // 2, ZN) * 2 + c
    toward = {UP: above, DOWN: below, FAR: far}

    def col(mr):
        return lax.rem(m + mr, KVH)

    def head_lanes(j):
        return pl.ds(pl.multiple_of(j * HD, HD), HD)

    local = []
    for i, hbm in enumerate((q_hbm, g_hbm)):
        for hp in range(2):
            lanes = pl.ds(hp * 256, 256)
            local.append((hbm.at[:, lanes], qg.at[POS[hp, 0], pl.ds(i * 128, 128)]))
    local.append((a_hbm, abuf))
    local.append((l_hbm, lbuf))
    local.append((k_hbm.at[:, head_lanes(m)], kv.at[0, 0]))
    local.append((v_hbm.at[:, head_lanes(m)], kv.at[1, 0]))
    local = [pltpu.make_async_copy(s, d, local_sem.at[i]) for i, (s, d) in enumerate(local)]
    for copy in local:
        copy.start()

    barrier = pltpu.get_barrier_semaphore()
    peers = [(r, col(mr)) for mr in range(1, KVH)]
    peers += [(other, m), (sibling, m), (above, m), (below, m), (far, m)]
    for peer in peers:
        pl.semaphore_signal(barrier, inc=1, device_id=peer, device_id_type=MESH)

    def a2a(mr, i):
        slot = KVH - mr
        return pltpu.make_async_remote_copy(
            src_ref=(k_hbm, v_hbm)[i].at[:, head_lanes(col(mr))],
            dst_ref=kv.at[i, slot],
            send_sem=a2a_send.at[i, mr],
            recv_sem=a2a_recv.at[slot // 4, i],
            device_id=(r, col(mr)),
            device_id_type=MESH,
        )

    def wait_a2a(g):
        for i in range(2):
            got = kv.at[i, pl.ds(4 * g + 1 - g, 3 + g)]
            pltpu.make_async_copy(got, got, a2a_recv.at[g, i]).wait()

    def relay(g):
        return pltpu.make_async_remote_copy(
            src_ref=kv.at[:, pl.ds(4 * g, 4)],
            dst_ref=kv.at[:, pl.ds(16 + 8 * g, 4)],
            send_sem=relay_send.at[g],
            recv_sem=relay_recv.at[g],
            device_id=(other, m),
            device_id_type=MESH,
        )

    def forward(xr, g):
        here, there = ((4 * g, 8 + 4 * g), (16 + 8 * g, 20 + 8 * g))[xr]
        return pltpu.make_async_remote_copy(
            src_ref=kv.at[:, pl.ds(here, 4)],
            dst_ref=kv.at[:, pl.ds(there, 4)],
            send_sem=fwd_send.at[xr, g],
            recv_sem=fwd_recv.at[xr, g],
            device_id=(sibling, m),
            device_id_type=MESH,
        )

    def turn(first, count):
        def one(s, _):
            kt[first + s] = kv[0, first + s].T
            return 0

        lax.fori_loop(0, count, one, 0)

    def start_forward(g):
        relay(g).wait_recv()
        forward(1, g).start()
        turn(16 + 8 * g, 4)

    def take_forward(g):
        forward(1, g).wait_recv()
        turn(20 + 8 * g, 4)

    def ring(d, hp, hop, part):
        slot = GATHER[d, hp][hop]
        landing = (slot + 1) % ZN if d == UP else (slot + ZN - 1) % ZN
        rows = pl.ds(0, ROWS)
        return pltpu.make_async_remote_copy(
            src_ref=qg.at[POS[hp, slot], rows],
            dst_ref=qg.at[POS[hp, landing], rows],
            send_sem=ring_send.at[d, hp, hop, part],
            recv_sem=ring_recv.at[d, hp, hop, part],
            device_id=(toward[d], m),
            device_id_type=MESH,
        )

    def pass_on(hp, hop, parts=(0,)):
        for part in parts:
            for d in (UP, DOWN):
                hops = len(GATHER[d, hp])
                if hop > 0 and hop <= hops:
                    ring(d, hp, hop - 1, part).wait_recv()
                if hop < hops:
                    ring(d, hp, hop, part).start()

    def zero(i, _):
        acc[i] = jnp.zeros((128, 256), F32)
        return 0

    for copy in local[:6]:
        copy.wait()

    lane = lax.broadcasted_iota(jnp.int32, (128, 128), 1)
    stats = jnp.zeros((128, 128), F32)
    for h in range(4):
        hp, hl = h // 2, h % 2
        grad = qg[POS[hp, 0], 128:256, hl * 128 : hl * 128 + 128].astype(F32)
        attn = abuf[:, h * 128 : h * 128 + 128].astype(F32)
        stats = jnp.where(lane == h, jnp.sum(grad * attn, axis=1, keepdims=True), stats)
    stats = stats.T
    row = lax.broadcasted_iota(jnp.int32, (16, 256), 0)
    stats = (lbuf[...] * LOG2E, stats)
    for hp in range(2):
        packed = jnp.zeros((16, 256), F32)
        for i in range(2):
            rest = jnp.concatenate([stats[i][2 * hp + hl : 2 * hp + hl + 1] for hl in range(2)], axis=1)
            for piece in range(3):
                part = rest.astype(BF16).astype(F32)
                packed = jnp.where(row == 3 * i + piece, part, packed)
                rest = rest - part
        qg[POS[hp, 0], 256:272, :] = packed.astype(BF16)

    pl.semaphore_wait(barrier, len(peers))
    pass_on(0, 0)
    for mr in reversed(range(1, KVH)):
        for i in range(2):
            a2a(mr, i).start()
    pass_on(1, 0)
    lax.fori_loop(0, 16, zero, 0)
    for copy in local[6:]:
        copy.wait()
    for g in range(2):
        wait_a2a(g)
        relay(g).start()
        forward(0, g).start()
        pass_on(g, 1)
    turn(0, 8)
    for g in range(2):
        forward(0, g).wait_recv()
    turn(8, 8)
    pass_on(0, 2)

    def reduce_copy(d, hp, slot):
        i = MSG[d, hp, slot]
        return pltpu.make_async_remote_copy(
            src_ref=sbuf.at[i],
            dst_ref=rbuf.at[i],
            send_sem=red_send.at[i],
            recv_sem=red_recv.at[i],
            device_id=(toward[d], m),
            device_id_type=MESH,
        )

    def send_sum(d, hp, slot):
        total = acc[POS[hp, slot]]
        before = (d, hp, slot + 1 if d == DOWN else slot - 1)
        if before in MSG and d != FAR:
            reduce_copy(*before).wait_recv()
            total = total + rbuf[MSG[before]].astype(F32)
        sbuf[MSG[d, hp, slot]] = total.astype(BF16)
        reduce_copy(d, hp, slot).start()

    def finish(hp):
        total = acc[POS[hp, 0]]
        for last in ((FAR, hp, 4), (DOWN, hp, 1), (UP, hp, 7)):
            reduce_copy(*last).wait_recv()
            total = total + rbuf[MSG[last]].astype(F32)
        total = total * SCALE
        for hl in range(2):
            h = 2 * hp + hl
            out_ref[:, h * 128 : h * 128 + 128] = total[:, hl * 128 : hl * 128 + 128].T

    def work(u, half):
        first = half * 16
        ks = kv[0, pl.ds(first, 16)].reshape(16 * 128, HD)
        vs = kv[1, pl.ds(first, 16)].reshape(16 * 128, HD)
        blocks = [qg[2 * u], qg[2 * u + 1]]
        qs = jnp.concatenate([b[0:128, i : i + 128] for b in blocks for i in (0, 128)], axis=0)
        gs = jnp.concatenate([b[128:256, i : i + 128] for b in blocks for i in (0, 128)], axis=0)
        st = jnp.concatenate([b[256:272] for b in blocks], axis=1).astype(F32)
        logs = st[0:1] + st[1:2] + st[2:3]
        dots = st[3:4] + st[4:5] + st[5:6]
        scores = lax.dot_general(ks, qs, NT, preferred_element_type=F32)
        probs = lax.dot_general(vs, gs, NT, preferred_element_type=F32)
        ds = (jnp.exp2(scores * (SCALE * LOG2E) - logs) * (probs - dots)).astype(BF16)
        keys = jnp.concatenate([kt[first + i] for i in range(16)], axis=1)
        part = lax.dot_general(keys, ds, NN, preferred_element_type=F32)
        acc[2 * u] += part[:, :256]
        acc[2 * u + 1] += part[:, 256:]

    events = {
        0: [(pass_on, 1, 2)],
        2: [(pass_on, 0, 3)],
        3: [(start_forward, 0)],
        4: [(pass_on, 1, 3)],
        5: [(start_forward, 1), (take_forward, 0)],
        6: [(take_forward, 1)],
        7: [(send_sum, UP, 0, 5), (send_sum, DOWN, 0, 3)],
        8: [(send_sum, UP, 1, 5), (send_sum, DOWN, 1, 3)],
        10: [(pass_on, 0, 4), (pass_on, 1, 4), (send_sum, UP, 0, 6), (send_sum, DOWN, 0, 2)],
        11: [(send_sum, UP, 1, 6), (send_sum, DOWN, 1, 2)],
        12: [(send_sum, FAR, 0, 4), (send_sum, FAR, 1, 4)],
        13: [(send_sum, UP, 0, 7), (send_sum, DOWN, 0, 1)],
        14: [(send_sum, UP, 1, 7), (send_sum, DOWN, 1, 1)],
    }

    def one_step(i, _):
        work(pick(i, STEP_UNIT), pick(i, STEP_HALF))
        for when, calls in events.items():
            @pl.when(i == when)
            def _(calls=calls):
                for call in calls:
                    call[0](*call[1:])
        return 0

    lax.fori_loop(0, len(STEP_UNIT), one_step, 0)
    finish(0)
    finish(1)

    for mr in range(1, KVH):
        for i in range(2):
            a2a(mr, i).wait_send()
    for g in range(2):
        relay(g).wait_send()
        for xr in range(2):
            forward(xr, g).wait_send()
    for (d, hp), hops in GATHER.items():
        for hop in range(len(hops)):
            for part in range(1):
                ring(d, hp, hop, part).wait_send()
    for message in MESSAGES:
        reduce_copy(*message).wait_send()


def body(queries, grad_out, attn_out, log_sum, memory_keys, memory_values):
    entries = memory_keys.shape[0] * memory_keys.shape[1]
    any_space = pl.BlockSpec(memory_space=pl.ANY)
    in_vmem = pl.BlockSpec(memory_space=pltpu.VMEM)
    return pl.pallas_call(
        kernel,
        out_shape=jax.ShapeDtypeStruct(queries.shape, F32),
        in_specs=[any_space] * 6,
        out_specs=in_vmem,
        scratch_shapes=[
            pltpu.VMEM((16, ROWS, 256), BF16),
            pltpu.VMEM((2, 32, 128, HD), BF16),
            pltpu.VMEM((32, HD, 128), BF16),
            pltpu.VMEM((16, HD, 256), F32),
            pltpu.VMEM((128, 512), BF16),
            pltpu.VMEM((4, 128), F32),
            pltpu.VMEM((len(MESSAGES), HD, 256), BF16),
            pltpu.VMEM((len(MESSAGES), HD, 256), BF16),
            pltpu.SemaphoreType.DMA((8,)),
            pltpu.SemaphoreType.DMA((2, KVH)),
            pltpu.SemaphoreType.DMA((2, 2)),
            pltpu.SemaphoreType.DMA((2,)),
            pltpu.SemaphoreType.DMA((2,)),
            pltpu.SemaphoreType.DMA((2, 2)),
            pltpu.SemaphoreType.DMA((2, 2)),
            pltpu.SemaphoreType.DMA((2, 2, 4, 2)),
            pltpu.SemaphoreType.DMA((2, 2, 4, 2)),
            pltpu.SemaphoreType.DMA((len(MESSAGES),)),
            pltpu.SemaphoreType.DMA((len(MESSAGES),)),
        ],
        compiler_params=pltpu.CompilerParams(
            collective_id=0, has_side_effects=True, vmem_limit_bytes=60 << 20
        ),
        cost_estimate=pl.CostEstimate(flops=12884901888, bytes_accessed=2 << 20, transcendentals=16777216),
    )(
        queries,
        grad_out,
        attn_out,
        log_sum.T,
        memory_keys.reshape(entries, KVH * HD),
        memory_values.reshape(entries, KVH * HD),
    )


def solution(mesh):
    return jax.shard_map(
        body,
        mesh=mesh,
        in_specs=(
            P("mrow", "mcol"),
            P("mrow", "mcol"),
            P("mrow", "mcol"),
            P("mrow", "mcol"),
            P("mrow", "mcol", None),
            P("mrow", "mcol", None),
        ),
        out_specs=P("mrow", "mcol"),
        check_vma=False,
    )
```

time: 72.3 us -> 59.9 us (0.83); the launches traced: 72.2 us -> 58.7 us
  Pallas kernels: 69 us -> 57 us
  local copies, waits for them, and re-layouts: 3.09 us -> 1.67 us
    pallas_call x1, Pallas kernels: 69 us -> 57 us  [body(): pl.pallas_call(kernel, out_shape=jax.ShapeDtypeStruct(queries.shape, F32)...]
    unnamed x4 -> x1, local copies, waits for them, and re-layouts: 3.09 us -> 1.67 us
where the time goes in v2:
time: 59.9 us; the launch traced here: 58.7 us
  Pallas kernels  57 us (95%)
  local copies, waits for them, and re-layouts  1.67 us (3%)
    pallas_call x1, Pallas kernels, body(): pl.pallas_call(kernel, out_shape=jax.ShapeDtypeStruct(queries.shape, F32)...  57 us
    unnamed x1, local copies, waits for them, and re-layouts  1.67 us

profile of v2, /device:TPU:16, one launch (start us, length us, event | category | flops | bytes accessed | tf_op | source)
XLA Modules:
  0.0 58.7 jit_solution(8721722727683318600)
XLA Ops:
  0.0 57.0 %shard_map.64 = f32[128,512]{1,0:T(8,128)} custom-call(bf16[128,512]{1,0:T(8,128)(2,1)} %q_hbm.1, bf16[128,512]{1,0:T(8,128)(2,1)} %g_hbm.1, bf16[128,512]{1,0:T(8,128)(2,1)} %a_hbm.1, f32[4,128]{1,0:T(4,128)} %bitcast.5, bf16[128,1024]{1,0:T(8,128)(2,1)} %bitcast.3, bf16[128,1024]{1,0:T(8,128)(2,1)} %bitcast.4), custom_call_target="tpu_custom_call" | custom-call | flops 12884901888 | bytes 2097152 | tf_op jit(solution)/shard_map/pallas_call | solution.py:305
  57.0 1.7 %copy.8 = f32[128,512]{1,0:T(8,128)} copy(f32[128,512]{1,0:T(8,128)} %shard_map.64) | data formatting | bytes 524288
